TPU v7x, 32 devices: a whole 2x2x4 slice. The times are simulated.
32 devices in a mesh: own: 16 (over z, x, core), pair: 2 (over y).
Axes of the slice: x: 2, y: 2, z: 4, core: 2. Of those that a mesh axis runs over, the one named last changes fastest.
Arguments:
- embeddings: float32 [32, 128, 1024], P('own'), as said below
- cluster_sizes: int32 [8], replicated, may hold values from 1 to 12, 32 in all
- row_counts: int32 [32], replicated, may hold values from 32 to 128, as said below
Outputs:
- near_sums: bfloat16 [32, 128, 1024], P('own', 'pair')
- log_masses: float32 [32, 128], P('own', 'pair')
Inputs may be any that keep to these rules, and one draw needn't show every extreme that they name: `row_counts`: some block has all 128 valid rows. `embeddings`: finite rows of nonzero norm.
All inputs are finite; a program needn't handle non-finite values.
Results may differ from a plain program's by a relative error of at most 0.01.
Values may be sent and summed in bfloat16 or wider, within the bound.
A program may use at most 64 MiB of HBM per device.

v0:
```python
import jax
import jax.numpy as jnp
from jax import lax
from jax.sharding import PartitionSpec as P

SPAN = 12


sharpness = 128.0
negative = -1e30


def passed_along(shard, axis, by):
    count = lax.axis_size(axis)
    pairs = [(i, i + by) for i in range(count) if 0 <= i + by < count]
    return lax.ppermute(shard, axis, pairs)


def unit_rows(values):
    squares = jnp.sum(values * values, axis=-1, keepdims=True)
    return (values * lax.rsqrt(squares + 1e-06)).astype(jnp.bfloat16)


def fold_in(running, row_top, row_total, partial_value):
    run_max, run_mass, run_sum = running
    new_max = jnp.maximum(run_max, row_top)
    old_scale = jnp.exp(run_max - new_max)
    new_scale = jnp.exp(row_top - new_max)
    return (
        new_max,
        run_mass * old_scale + row_total * new_scale,
        run_sum * old_scale[..., None] + partial_value * new_scale[..., None],
    )


def combine_states(first_state, second_state):
    return fold_in(first_state, second_state[0], second_state[1], second_state[2])


def row_stats(scores, kept, key_rows):
    scores = jnp.where(kept, scores, negative)
    row_top = jnp.max(scores, axis=1)
    weight = jnp.where(kept, jnp.exp(scores - row_top[:, None]), 0.0)
    partial_value = jnp.dot(
        weight.astype(jnp.bfloat16), key_rows, preferred_element_type=jnp.float32
    )
    return (row_top, jnp.sum(weight, axis=1), partial_value)


def pick_entry(table, position):
    places = jnp.arange(table.shape[0], dtype=jnp.int32)
    return jnp.sum(jnp.where(places == position, table, 0))


def empty_state(row_total, feature_count):
    return (
        jnp.full((row_total,), negative, jnp.float32),
        jnp.zeros((row_total,), jnp.float32),
        jnp.zeros((row_total, feature_count), jnp.float32),
    )


def stack_states(states):
    return tuple((jnp.stack([state[field] for state in states]) for field in range(3)))


def own_rows(stacked, slice_rows, pair_count):
    run_max, run_mass, run_sum = stacked
    local_blocks = run_max.shape[0]
    feature_count = run_sum.shape[2]
    arrived = (
        lax.all_to_all(
            run_max.reshape(local_blocks, pair_count, slice_rows),
            "pair",
            split_axis=1,
            concat_axis=1,
            tiled=True,
        ),
        lax.all_to_all(
            run_mass.reshape(local_blocks, pair_count, slice_rows),
            "pair",
            split_axis=1,
            concat_axis=1,
            tiled=True,
        ),
        lax.all_to_all(
            run_sum.reshape(local_blocks, pair_count, slice_rows, feature_count),
            "pair",
            split_axis=1,
            concat_axis=1,
            tiled=True,
        ),
    )
    new_max = jnp.max(arrived[0], axis=1)
    scales = jnp.exp(arrived[0] - new_max[:, None, :])
    return (
        new_max,
        jnp.sum(arrived[1] * scales, axis=1),
        jnp.sum(arrived[2] * scales[..., None], axis=1),
    )


def body(embeddings, cluster_sizes, row_counts):
    normed = unit_rows(embeddings)
    local_blocks, block_rows, feature_count = normed.shape
    pair_count = lax.axis_size("pair")
    own_count = lax.axis_size("own")
    block_total = own_count * local_blocks
    slice_rows = block_rows // pair_count
    own_index = lax.axis_index("own")
    slice_start = lax.axis_index("pair") * slice_rows
    my_slice = lax.dynamic_slice_in_dim(normed, slice_start, slice_rows, 1)
    cluster_start = jnp.cumsum(cluster_sizes) - cluster_sizes
    block_ids = jnp.arange(block_total, dtype=jnp.int32)
    owner_cluster = (
        jnp.sum((block_ids[:, None] >= cluster_start[None, :]).astype(jnp.int32), axis=1) - 1
    )
    full_rows = jnp.arange(block_rows, dtype=jnp.int32)
    my_rows = slice_start + jnp.arange(slice_rows, dtype=jnp.int32)
    offset_count = (SPAN + local_blocks - 2) // local_blocks

    def block_of(owner, local):
        return owner * local_blocks + local

    def linked_to(query_block, source):
        inside = (source >= 0) & (source < block_total)
        return inside & (
            pick_entry(owner_cluster, source) == pick_entry(owner_cluster, query_block)
        )

    def key_mask(query_block, source):
        valid_keys = my_rows[None, :] < pick_entry(row_counts, source)
        not_self = (query_block != source) | (full_rows[:, None] != my_rows[None, :])
        return linked_to(query_block, source) & valid_keys & not_self

    def tile_scores(queries, key_rows):
        return sharpness * jnp.dot(queries, key_rows.T, preferred_element_type=jnp.float32)

    running = [empty_state(block_rows, feature_count) for local in range(local_blocks)]
    for local in range(local_blocks):
        query_block = block_of(own_index, local)
        for other in range(local_blocks):
            source = block_of(own_index, other)
            row_top, row_total, partial_value = row_stats(
                tile_scores(normed[local], my_slice[other]),
                key_mask(query_block, source),
                my_slice[other],
            )
            running[local] = fold_in(running[local], row_top, row_total, partial_value)
    column_state = [empty_state(slice_rows, feature_count) for local in range(local_blocks)]
    for offset in range(1, offset_count + 1):
        earlier = passed_along(my_slice, "own", offset)
        back_states = [empty_state(slice_rows, feature_count) for local in range(local_blocks)]
        for local in range(local_blocks):
            query_block = block_of(own_index, local)
            query_valid = full_rows < pick_entry(row_counts, query_block)
            for other in range(local_blocks):
                source = block_of(own_index - offset, other)
                scores = tile_scores(normed[local], earlier[other])
                row_top, row_total, partial_value = row_stats(
                    scores, key_mask(query_block, source), earlier[other]
                )
                running[local] = fold_in(running[local], row_top, row_total, partial_value)
                back_mask = (
                    linked_to(query_block, source) & query_valid[None, :] & (my_rows[:, None] >= 0)
                )
                back_top, back_total, back_sum = row_stats(scores.T, back_mask, normed[local])
                back_states[other] = fold_in(back_states[other], back_top, back_total, back_sum)
        stacked_back = stack_states(back_states)
        returned = passed_along((stacked_back[0], stacked_back[1], stacked_back[2]), "own", -offset)
        later_inside = own_index + offset < own_count
        for local in range(local_blocks):
            column_state[local] = fold_in(
                column_state[local],
                jnp.where(later_inside, returned[0][local], negative),
                jnp.where(later_inside, returned[1][local], 0.0),
                jnp.where(later_inside, returned[2][local], 0.0),
            )
    reduced = own_rows(stack_states(running), slice_rows, pair_count)
    result_state = combine_states(reduced, stack_states(column_state))
    run_max, run_mass, run_sum = result_state
    my_counts = jnp.stack(
        [pick_entry(row_counts, block_of(own_index, local)) for local in range(local_blocks)]
    )
    row_valid = my_rows[None, :] < my_counts[:, None]
    near_sums = jnp.where(row_valid[..., None], run_sum / run_mass[..., None], 0.0).astype(
        jnp.bfloat16
    )
    log_masses = jnp.where(row_valid, run_max + jnp.log(run_mass), 0.0)
    return (near_sums, log_masses)


def solution(mesh):
    placed = (P("own", None, None), P(), P())
    return jax.shard_map(
        body,
        mesh=mesh,
        in_specs=placed,
        out_specs=(P("own", "pair", None), P("own", "pair")),
        check_vma=False,
    )
```

profile of v0, /device:TPU:6, one launch (start us, length us, event | category | flops | bytes accessed | tf_op | source)
XLA Modules:
  0.0 333.7 jit_solution(10809291704599679046)
XLA Ops:
  0.6 1.5 multiply_reduce_fusion.1
  2.3 1.9 collective-permute-start
  4.3 4.5 %collective-permute-start.5 = (bf16[2,64,1024]{2,1,0:T(8,128)(2,1)S(1)}, bf16[2,64,1024]{2,1,0:T(8,128)(2,1)S(1)}, u32[]{:S(2)}, u32[]{:S(2)}) collective-permute-start(bf16[2,64,1024]{2,1,0:T(8,128)(2,1)S(1)} %constant_dynamic-slice_fusion), channel_id=1, source_target_pairs={{0,12},{2,14},{4,16},{6,18},{8,20},{10,22},{12,24},{14,26},{16,28}... | collective-permute-start | bytes 786440 | tf_op jit(solution)/shard_map/ppermute | solution.py:16
  8.7 3.4 %collective-permute-start.1 = (bf16[2,64,1024]{2,1,0:T(8,128)(2,1)S(1)}, bf16[2,64,1024]{2,1,0:T(8,128)(2,1)S(1)}, u32[]{:S(2)}, u32[]{:S(2)}) collective-permute-start(bf16[2,64,1024]{2,1,0:T(8,128)(2,1)S(1)} %constant_dynamic-slice_fusion), channel_id=1, source_target_pairs={{0,4},{2,6},{4,8},{6,10},{8,12},{10,14},{12,16},{14,18},{16,20},{1... | collective-permute-start | bytes 786440 | tf_op jit(solution)/shard_map/ppermute | solution.py:16
  12.2 4.1 %collective-permute-start.2 = (bf16[2,64,1024]{2,1,0:T(8,128)(2,1)S(1)}, bf16[2,64,1024]{2,1,0:T(8,128)(2,1)S(1)}, u32[]{:S(2)}, u32[]{:S(2)}) collective-permute-start(bf16[2,64,1024]{2,1,0:T(8,128)(2,1)S(1)} %constant_dynamic-slice_fusion), channel_id=1, source_target_pairs={{0,6},{2,8},{4,10},{6,12},{8,14},{10,16},{12,18},{14,20},{16,22},{... | collective-permute-start | bytes 786440 | tf_op jit(solution)/shard_map/ppermute | solution.py:16
  72.3 1.8 broadcast_and_fusion.5
  75.6 1.8 pad_add_fusion
  81.4 1.8 broadcast_and_fusion.7
  118.2 3.6 %collective-permute-start.6 = (f32[2,64]{1,0:T(2,128)}, f32[2,64]{1,0:T(2,128)}, u32[]{:S(2)}, u32[]{:S(2)}) collective-permute-start(f32[2,64]{1,0:T(2,128)} %pad_maximum_fusion.9), channel_id=1, source_target_pairs={{2,0},{4,2},{6,4},{8,6},{10,8},{12,10},{14,12},{16,14},{18,16},{20... | collective-permute-start | bytes 1544 | tf_op jit(solution)/shard_map/ppermute | solution.py:16
  132.5 1.4 collective-permute-start.9
  161.8 3.7 %all-to-all-start.1 = ((f32[2,1,128]{2,1,0:T(1,128)}), f32[2,1,128]{2,1,0:T(1,128)S(1)}, u32[]{:S(2)}, u32[]{:S(2)}) async-start(f32[2,1,128]{2,1,0:T(1,128)} %reshape.4530), calls=%async_computation.1 | async-start | bytes 2048 | tf_op jit(solution)/shard_map/all_to_all | solution.py:72
  216.5 3.3 %all-to-all-start.2 = ((f32[2,1,128]{2,1,0:T(1,128)}), f32[2,1,128]{2,1,0:T(1,128)S(1)}, u32[]{:S(2)}, u32[]{:S(2)}) async-start(f32[2,1,128]{2,1,0:T(1,128)} %reshape.4532), calls=%async_computation.2 | async-start | bytes 2048 | tf_op jit(solution)/shard_map/all_to_all | solution.py:79
  221.9 1.9 collective-permute-start.7
  223.8 1.9 collective-permute-start.18
  225.7 3.6 %all-to-all-start = ((f32[2,2,64,1024]{3,2,0,1:T(8,128)}), f32[2,2,64,1024]{3,2,0,1:T(8,128)S(1)}, u32[]{:S(2)}, u32[]{:S(2)}) async-start(f32[2,2,64,1024]{3,2,0,1:T(8,128)} %pad_maximum_fusion), calls=%async_computation | async-start | bytes 2097152 | tf_op jit(solution)/shard_map/all_to_all | solution.py:86
  230.7 1.9 collective-permute-start.19
  237.9 1.9 collective-permute-start.12
  240.0 1.9 collective-permute-start.13
  245.7 3.6 %collective-permute-done.23 = f32[2,64]{1,0:T(2,128)S(1)} collective-permute-done((f32[2,64]{1,0:T(2,128)S(1)}, f32[2,64]{1,0:T(2,128)S(1)}, u32[]{:S(2)}, u32[]{:S(2)}) %collective-permute-start.23) | collective-permute-done | bytes 544 | tf_op jit(solution)/shard_map/ppermute | solution.py:16
  254.8 9.9 %collective-permute-done.13 = f32[2,64,1024]{2,1,0:T(8,128)S(1)} collective-permute-done((f32[2,64,1024]{2,1,0:T(8,128)}, f32[2,64,1024]{2,1,0:T(8,128)S(1)}, u32[]{:S(2)}, u32[]{:S(2)}) %collective-permute-start.13) | collective-permute-done | bytes 524320 | tf_op jit(solution)/shard_map/ppermute | solution.py:16
  264.7 7.1 %collective-permute-done.14 = f32[2,64,1024]{2,1,0:T(8,128)S(1)} collective-permute-done((f32[2,64,1024]{2,1,0:T(8,128)}, f32[2,64,1024]{2,1,0:T(8,128)S(1)}, u32[]{:S(2)}, u32[]{:S(2)}) %collective-permute-start.14) | collective-permute-done | bytes 524320 | tf_op jit(solution)/shard_map/ppermute | solution.py:16
  271.8 1.8 collective-permute-done.15
  273.6 3.7 %collective-permute-done.16 = f32[2,64,1024]{2,1,0:T(8,128)} collective-permute-done((f32[2,64,1024]{2,1,0:T(8,128)}, f32[2,64,1024]{2,1,0:T(8,128)}, u32[]{:S(2)}, u32[]{:S(2)}) %collective-permute-start.16) | collective-permute-done | bytes 524320 | tf_op jit(solution)/shard_map/ppermute | solution.py:16
  277.4 52.8 %collective-permute-done.17 = f32[2,64,1024]{2,1,0:T(8,128)} collective-permute-done((f32[2,64,1024]{2,1,0:T(8,128)}, f32[2,64,1024]{2,1,0:T(8,128)}, u32[]{:S(2)}, u32[]{:S(2)}) %collective-permute-start.17) | collective-permute-done | bytes 524320 | tf_op jit(solution)/shard_map/ppermute | solution.py:16
  (683 shorter events, 172.1 us)
Async XLA Ops:
  2.3 83.5 %collective-permute-start = (bf16[2,64,1024]{2,1,0:T(8,128)(2,1)S(1)}, bf16[2,64,1024]{2,1,0:T(8,128)(2,1)S(1)}, u32[]{:S(2)}, u32[]{:S(2)}) collective-permute-start(bf16[2,64,1024]{2,1,0:T(8,128)(2,1)S(1)} %constant_dynamic-slice_fusion), channel_id=1, source_target_pairs={{0,2},{2,4},{4,6},{6,8},{8,10},{10,12},{12,14},{14,16},{16,18},{18... | collective-permute-start | bytes 786440 | tf_op jit(solution)/shard_map/ppermute | solution.py:16
  4.3 83.1 %collective-permute-start.5 = (bf16[2,64,1024]{2,1,0:T(8,128)(2,1)S(1)}, bf16[2,64,1024]{2,1,0:T(8,128)(2,1)S(1)}, u32[]{:S(2)}, u32[]{:S(2)}) collective-permute-start(bf16[2,64,1024]{2,1,0:T(8,128)(2,1)S(1)} %constant_dynamic-slice_fusion), channel_id=1, source_target_pairs={{0,12},{2,14},{4,16},{6,18},{8,20},{10,22},{12,24},{14,26},{16,28}... | collective-permute-start | bytes 786440 | tf_op jit(solution)/shard_map/ppermute | solution.py:16
  8.7 75.1 %collective-permute-start.1 = (bf16[2,64,1024]{2,1,0:T(8,128)(2,1)S(1)}, bf16[2,64,1024]{2,1,0:T(8,128)(2,1)S(1)}, u32[]{:S(2)}, u32[]{:S(2)}) collective-permute-start(bf16[2,64,1024]{2,1,0:T(8,128)(2,1)S(1)} %constant_dynamic-slice_fusion), channel_id=1, source_target_pairs={{0,4},{2,6},{4,8},{6,10},{8,12},{10,14},{12,16},{14,18},{16,20},{1... | collective-permute-start | bytes 786440 | tf_op jit(solution)/shard_map/ppermute | solution.py:16
  12.2 74.8 %collective-permute-start.2 = (bf16[2,64,1024]{2,1,0:T(8,128)(2,1)S(1)}, bf16[2,64,1024]{2,1,0:T(8,128)(2,1)S(1)}, u32[]{:S(2)}, u32[]{:S(2)}) collective-permute-start(bf16[2,64,1024]{2,1,0:T(8,128)(2,1)S(1)} %constant_dynamic-slice_fusion), channel_id=1, source_target_pairs={{0,6},{2,8},{4,10},{6,12},{8,14},{10,16},{12,18},{14,20},{16,22},{... | collective-permute-start | bytes 786440 | tf_op jit(solution)/shard_map/ppermute | solution.py:16
  16.3 70.0 %collective-permute-start.3 = (bf16[2,64,1024]{2,1,0:T(8,128)(2,1)S(1)}, bf16[2,64,1024]{2,1,0:T(8,128)(2,1)S(1)}, u32[]{:S(2)}, u32[]{:S(2)}) collective-permute-start(bf16[2,64,1024]{2,1,0:T(8,128)(2,1)S(1)} %constant_dynamic-slice_fusion), channel_id=1, source_target_pairs={{0,8},{2,10},{4,12},{6,14},{8,16},{10,18},{12,20},{14,22},{16,24},... | collective-permute-start | bytes 786440 | tf_op jit(solution)/shard_map/ppermute | solution.py:16
  118.2 103.0 %collective-permute-start.6 = (f32[2,64]{1,0:T(2,128)}, f32[2,64]{1,0:T(2,128)}, u32[]{:S(2)}, u32[]{:S(2)}) collective-permute-start(f32[2,64]{1,0:T(2,128)} %pad_maximum_fusion.9), channel_id=1, source_target_pairs={{2,0},{4,2},{6,4},{8,6},{10,8},{12,10},{14,12},{16,14},{18,16},{20... | collective-permute-start | bytes 1544 | tf_op jit(solution)/shard_map/ppermute | solution.py:16
  123.5 100.2 %collective-permute-start.8 = (f32[2,64]{1,0:T(2,128)}, f32[2,64]{1,0:T(2,128)}, u32[]{:S(2)}, u32[]{:S(2)}) collective-permute-start(f32[2,64]{1,0:T(2,128)} %pad_maximum_fusion.11), channel_id=1, source_target_pairs={{6,0},{8,2},{10,4},{12,6},{14,8},{16,10},{18,12},{20,14},{22,16},{... | collective-permute-start | bytes 1544 | tf_op jit(solution)/shard_map/ppermute | solution.py:16
  126.5 103.6 %collective-permute-start.10 = (f32[2,64]{1,0:T(2,128)}, f32[2,64]{1,0:T(2,128)}, u32[]{:S(2)}, u32[]{:S(2)}) collective-permute-start(f32[2,64]{1,0:T(2,128)} %pad_maximum_fusion.13), channel_id=1, source_target_pairs={{10,0},{12,2},{14,4},{16,6},{18,8},{20,10},{22,12},{24,14},{26,16}... | collective-permute-start | bytes 1544 | tf_op jit(solution)/shard_map/ppermute | solution.py:16
  129.5 103.1 %collective-permute-start.11 = (f32[2,64]{1,0:T(2,128)}, f32[2,64]{1,0:T(2,128)S(1)}, u32[]{:S(2)}, u32[]{:S(2)}) collective-permute-start(f32[2,64]{1,0:T(2,128)} %pad_maximum_fusion.14), channel_id=1, source_target_pairs={{12,0},{14,2},{16,4},{18,6},{20,8},{22,10},{24,12},{26,14},{28,16}... | collective-permute-start | bytes 1544 | tf_op jit(solution)/shard_map/ppermute | solution.py:16
  132.5 101.4 %collective-permute-start.9 = (f32[2,64]{1,0:T(2,128)}, f32[2,64]{1,0:T(2,128)S(1)}, u32[]{:S(2)}, u32[]{:S(2)}) collective-permute-start(f32[2,64]{1,0:T(2,128)} %pad_maximum_fusion.12), channel_id=1, source_target_pairs={{8,0},{10,2},{12,4},{14,6},{16,8},{18,10},{20,12},{22,14},{24,16},... | collective-permute-start | bytes 1544 | tf_op jit(solution)/shard_map/ppermute | solution.py:16
  161.8 54.6 %all-to-all-start.1 = ((f32[2,1,128]{2,1,0:T(1,128)}), f32[2,1,128]{2,1,0:T(1,128)S(1)}, u32[]{:S(2)}, u32[]{:S(2)}) async-start(f32[2,1,128]{2,1,0:T(1,128)} %reshape.4530), calls=%async_computation.1 | async-start | bytes 2048 | tf_op jit(solution)/shard_map/all_to_all | solution.py:72
  216.5 9.2 %all-to-all-start.2 = ((f32[2,1,128]{2,1,0:T(1,128)}), f32[2,1,128]{2,1,0:T(1,128)S(1)}, u32[]{:S(2)}, u32[]{:S(2)}) async-start(f32[2,1,128]{2,1,0:T(1,128)} %reshape.4532), calls=%async_computation.2 | async-start | bytes 2048 | tf_op jit(solution)/shard_map/all_to_all | solution.py:79
  221.9 13.4 %collective-permute-start.7 = (f32[2,64]{1,0:T(2,128)S(1)}, f32[2,64]{1,0:T(2,128)S(1)}, u32[]{:S(2)}, u32[]{:S(2)}) collective-permute-start(f32[2,64]{1,0:T(2,128)S(1)} %copy-done.89), channel_id=1, source_target_pairs={{4,0},{6,2},{8,4},{10,6},{12,8},{14,10},{16,12},{18,14},{20,16},{2... | collective-permute-start | bytes 1544 | tf_op jit(solution)/shard_map/ppermute | solution.py:16
  223.8 12.7 %collective-permute-start.18 = (f32[2,64]{1,0:T(2,128)S(1)}, f32[2,64]{1,0:T(2,128)S(1)}, u32[]{:S(2)}, u32[]{:S(2)}) collective-permute-start(f32[2,64]{1,0:T(2,128)S(1)} %copy-done.88), channel_id=1, source_target_pairs={{2,0},{4,2},{6,4},{8,6},{10,8},{12,10},{14,12},{16,14},{18,16},{20... | collective-permute-start | bytes 1544 | tf_op jit(solution)/shard_map/ppermute | solution.py:16
  225.7 28.9 %all-to-all-start = ((f32[2,2,64,1024]{3,2,0,1:T(8,128)}), f32[2,2,64,1024]{3,2,0,1:T(8,128)S(1)}, u32[]{:S(2)}, u32[]{:S(2)}) async-start(f32[2,2,64,1024]{3,2,0,1:T(8,128)} %pad_maximum_fusion), calls=%async_computation | async-start | bytes 2097152 | tf_op jit(solution)/shard_map/all_to_all | solution.py:86
  233.9 9.1 %collective-permute-start.21 = (f32[2,64]{1,0:T(2,128)S(1)}, f32[2,64]{1,0:T(2,128)S(1)}, u32[]{:S(2)}, u32[]{:S(2)}) collective-permute-start(f32[2,64]{1,0:T(2,128)S(1)} %copy-done.85), channel_id=1, source_target_pairs={{8,0},{10,2},{12,4},{14,6},{16,8},{18,10},{20,12},{22,14},{24,16},... | collective-permute-start | bytes 1544 | tf_op jit(solution)/shard_map/ppermute | solution.py:16
  235.2 9.1 %collective-permute-start.22 = (f32[2,64]{1,0:T(2,128)S(1)}, f32[2,64]{1,0:T(2,128)S(1)}, u32[]{:S(2)}, u32[]{:S(2)}) collective-permute-start(f32[2,64]{1,0:T(2,128)S(1)} %pad_maximum_fusion.20), channel_id=1, source_target_pairs={{10,0},{12,2},{14,4},{16,6},{18,8},{20,10},{22,12},{24,14},{26,16}... | collective-permute-start | bytes 1544 | tf_op jit(solution)/shard_map/ppermute | solution.py:16
  236.5 12.7 %collective-permute-start.23 = (f32[2,64]{1,0:T(2,128)S(1)}, f32[2,64]{1,0:T(2,128)S(1)}, u32[]{:S(2)}, u32[]{:S(2)}) collective-permute-start(f32[2,64]{1,0:T(2,128)S(1)} %pad_maximum_fusion.21), channel_id=1, source_target_pairs={{12,0},{14,2},{16,4},{18,6},{20,8},{22,10},{24,12},{26,14},{28,16}... | collective-permute-start | bytes 1544 | tf_op jit(solution)/shard_map/ppermute | solution.py:16
  237.9 14.2 %collective-permute-start.12 = (f32[2,64,1024]{2,1,0:T(8,128)}, f32[2,64,1024]{2,1,0:T(8,128)S(1)}, u32[]{:S(2)}, u32[]{:S(2)}) collective-permute-start(f32[2,64,1024]{2,1,0:T(8,128)} %pad_maximum_fusion.1), channel_id=1, source_target_pairs={{2,0},{4,2},{6,4},{8,6},{10,8},{12,10},{14,12},{16,14},{18,16},{20... | collective-permute-start | bytes 1572872 | tf_op jit(solution)/shard_map/ppermute | solution.py:16
  240.0 24.7 %collective-permute-start.13 = (f32[2,64,1024]{2,1,0:T(8,128)}, f32[2,64,1024]{2,1,0:T(8,128)S(1)}, u32[]{:S(2)}, u32[]{:S(2)}) collective-permute-start(f32[2,64,1024]{2,1,0:T(8,128)} %pad_maximum_fusion.2), channel_id=1, source_target_pairs={{4,0},{6,2},{8,4},{10,6},{12,8},{14,10},{16,12},{18,14},{20,16},{2... | collective-permute-start | bytes 1572872 | tf_op jit(solution)/shard_map/ppermute | solution.py:16
  243.1 28.8 %collective-permute-start.14 = (f32[2,64,1024]{2,1,0:T(8,128)}, f32[2,64,1024]{2,1,0:T(8,128)S(1)}, u32[]{:S(2)}, u32[]{:S(2)}) collective-permute-start(f32[2,64,1024]{2,1,0:T(8,128)} %pad_maximum_fusion.3), channel_id=1, source_target_pairs={{6,0},{8,2},{10,4},{12,6},{14,8},{16,10},{18,12},{20,14},{22,16},{... | collective-permute-start | bytes 1572872 | tf_op jit(solution)/shard_map/ppermute | solution.py:16
  244.4 29.3 %collective-permute-start.15 = (f32[2,64,1024]{2,1,0:T(8,128)}, f32[2,64,1024]{2,1,0:T(8,128)S(1)}, u32[]{:S(2)}, u32[]{:S(2)}) collective-permute-start(f32[2,64,1024]{2,1,0:T(8,128)} %pad_maximum_fusion.4), channel_id=1, source_target_pairs={{8,0},{10,2},{12,4},{14,6},{16,8},{18,10},{20,12},{22,14},{24,16},... | collective-permute-start | bytes 1572872 | tf_op jit(solution)/shard_map/ppermute | solution.py:16
  249.3 28.1 %collective-permute-start.16 = (f32[2,64,1024]{2,1,0:T(8,128)}, f32[2,64,1024]{2,1,0:T(8,128)}, u32[]{:S(2)}, u32[]{:S(2)}) collective-permute-start(f32[2,64,1024]{2,1,0:T(8,128)} %pad_maximum_fusion.5), channel_id=1, source_target_pairs={{10,0},{12,2},{14,4},{16,6},{18,8},{20,10},{22,12},{24,14},{26,16}... | collective-permute-start | bytes 1572872 | tf_op jit(solution)/shard_map/ppermute | solution.py:16
  252.1 78.1 %collective-permute-start.17 = (f32[2,64,1024]{2,1,0:T(8,128)}, f32[2,64,1024]{2,1,0:T(8,128)}, u32[]{:S(2)}, u32[]{:S(2)}) collective-permute-start(f32[2,64,1024]{2,1,0:T(8,128)} %pad_maximum_fusion.6), channel_id=1, source_target_pairs={{12,0},{14,2},{16,4},{18,6},{20,8},{22,10},{24,12},{26,14},{28,16}... | collective-permute-start | bytes 1572872 | tf_op jit(solution)/shard_map/ppermute | solution.py:16
  (193 other events, 837.6 us)
where the time goes:
time: 336 us; the launch traced here: 334 us
  waiting for transfers between devices  80.4 us (24%)
  local copies, waits for them, and re-layouts  67.5 us (20%)
  other arithmetic  67.5 us (20%)
  starting transfers between devices  56 us (17%)
  between operations  36.5 us (11%)
  matrix products  25.7 us (8%)
    ppermute x24, waiting for transfers between devices, passed_along(): return lax.ppermute(shard, axis, pairs)  80.4 us
    ppermute x24, starting transfers between devices, passed_along(): return lax.ppermute(shard, axis, pairs)  45.3 us
    unnamed x384, local copies, waits for them, and re-layouts  43 us
    reduce_sum x28, local copies, waits for them, and re-layouts, row_stats(): return (row_top, jnp.sum(weight, axis=1), partial_value)  18.3 us
    dot_general x52, matrix products, row_stats(): jnp.dot(weight.astype(jnp.bfloat16), key_rows, preferred_element_type=jnp...  16.1 us
    and x14, other arithmetic, body(): linked_to(query_block, source) & query_valid[None, :]  15 us
    another operation x21, other arithmetic, stack_states(): jnp.stack([state[field] for state in states])  11.9 us
    dot_general x28, matrix products, tile_scores(): jnp.dot(queries, key_rows.T, preferred_element_type=jnp.float32)  9.66 us
  transfers between devices with their start and end apart: 27, of which 8 were waited for; matrix products, arithmetic and copies ran while one was open for 29% of the time, Pallas kernels for 0%

commit v1 on v0

--- a/solution.py
+++ b/solution.py
@@ -1,6 +1,10 @@
+import functools
+
 import jax
 import jax.numpy as jnp
 from jax import lax
+from jax.experimental import pallas as pl
+from jax.experimental.pallas import tpu as pltpu
 from jax.sharding import PartitionSpec as P
 
 SPAN = 12
@@ -190,10 +194,437 @@
     return (near_sums, log_masses)
 
 
+MESH = pl.DeviceIdType.MESH
+
+
+def kernel(
+    groups, blocks, rows, slice_rows,
+    sizes_ref, counts_ref, emb_ref, near_ref, mass_ref,
+    queries, keys, top, mass, total,
+    chip_out, chip_in, chip_stats_out, chip_stats_in,
+    pair_out, pair_in, pair_stats_out, pair_stats_in,
+    share_send, share_recv, direct_send, key_recv, relay_send,
+    chip_send, chip_recv, chip_stats_send, chip_stats_recv,
+    pair_send, pair_recv, pair_stats_send, pair_stats_recv,
+):
+    width = emb_ref.shape[2]
+    mine = lax.axis_index("own")
+    half = lax.axis_index("pair")
+    group, core = mine // 2, mine % 2
+    lane_x = group % 2
+    toward = 1 - 2 * lane_x
+    sibling = mine + 1 - 2 * core
+    across = group + toward
+    ahead, behind = group + 2 * toward, group - 2 * toward
+    has_ahead = (ahead >= 0) & (ahead < groups)
+    has_behind = (behind >= 0) & (behind < groups)
+    behind2 = group - 4 * toward
+    has_behind2 = (behind2 >= 0) & (behind2 < groups)
+    zero_slot = 3
+    slots = 2 * blocks
+    half_rows = rows // 2
+    query_rows = slots * rows
+
+    def device(group_index, core_index):
+        return (group_index * 2 + core_index, half)
+
+    partner = (mine, 1 - half)
+
+    barrier = pltpu.get_barrier_semaphore()
+
+    def greet(target):
+        pl.semaphore_signal(barrier, inc=1, device_id=target, device_id_type=MESH)
+
+    greet(device(group, 1 - core))
+    greet(partner)
+    for other_core in range(2):
+        greet(device(across, other_core))
+
+    @pl.when(has_ahead)
+    def _():
+        for other_core in range(2):
+            greet(device(ahead, other_core))
+
+    @pl.when(has_behind)
+    def _():
+        for other_core in range(2):
+            greet(device(behind, other_core))
+
+    for local in range(blocks):
+        values = emb_ref[local]
+        squares = jnp.sum(values * values, axis=-1, keepdims=True)
+        queries[core * blocks + local] = (values * lax.rsqrt(squares + 1e-06)).astype(jnp.bfloat16)
+
+    own_blocks = pl.ds(core * blocks, blocks)
+
+    def key_rows(core_index):
+        return pl.ds(pl.multiple_of((half * 2 + core_index) * slice_rows, slice_rows), slice_rows)
+
+    share = pltpu.make_async_remote_copy(
+        src_ref=queries.at[own_blocks],
+        dst_ref=queries.at[own_blocks],
+        send_sem=share_send.at[0],
+        recv_sem=share_recv.at[0],
+        device_id=device(group, 1 - core),
+        device_id_type=MESH,
+    )
+    share_in = pltpu.make_async_remote_copy(
+        src_ref=queries.at[pl.ds((1 - core) * blocks, blocks)],
+        dst_ref=queries.at[pl.ds((1 - core) * blocks, blocks)],
+        send_sem=share_send.at[0],
+        recv_sem=share_recv.at[0],
+        device_id=device(group, 1 - core),
+        device_id_type=MESH,
+    )
+
+    def direct(place, target, slot, other_core):
+        return pltpu.make_async_remote_copy(
+            src_ref=queries.at[own_blocks, key_rows(other_core)],
+            dst_ref=keys.at[slot, core],
+            send_sem=direct_send.at[place, other_core],
+            recv_sem=key_recv.at[slot, core],
+            device_id=device(target, other_core),
+            device_id_type=MESH,
+        )
+
+    def relay(place, source_offset, target, target_offset, part):
+        return pltpu.make_async_remote_copy(
+            src_ref=keys.at[zero_slot + source_offset, part],
+            dst_ref=keys.at[zero_slot + target_offset, part],
+            send_sem=relay_send.at[place, part],
+            recv_sem=key_recv.at[zero_slot + target_offset, part],
+            device_id=device(target, core),
+            device_id_type=MESH,
+        )
+
+    def arrived(offset, part):
+        slot = zero_slot + offset
+        pltpu.make_async_remote_copy(
+            src_ref=keys.at[slot, part],
+            dst_ref=keys.at[slot, part],
+            send_sem=relay_send.at[0, part],
+            recv_sem=key_recv.at[slot, part],
+            device_id=device(across, core),
+            device_id_type=MESH,
+        ).wait_recv()
+
+    def direct_across(other_core):
+        return direct(0, across, zero_slot - toward, other_core)
+
+    def direct_ahead(other_core):
+        return direct(1, ahead, zero_slot - 2 * toward, other_core)
+
+    def direct_behind(other_core):
+        return direct(2, behind, zero_slot + 2 * toward, other_core)
+
+    def relay_across(part):
+        return relay(0, 2 * toward, across, toward, part)
+
+    def relay_behind(part):
+        return relay(1, toward, behind, 3 * toward, part)
+
+    def relay_ahead(part):
+        return relay(2, -toward, ahead, -3 * toward, part)
+
+    neighbours = 4 + 2 * has_ahead.astype(jnp.int32) + 2 * has_behind.astype(jnp.int32)
+    pl.semaphore_wait(barrier, neighbours)
+
+    for other_core in range(2):
+        direct_across(other_core).start()
+
+        @pl.when(has_ahead)
+        def _():
+            direct_ahead(other_core).start()
+
+        @pl.when(has_behind)
+        def _():
+            direct_behind(other_core).start()
+
+    share.start()
+
+    starts = []
+    so_far = jnp.int32(0)
+    for cluster in range(sizes_ref.shape[0]):
+        starts.append(so_far)
+        so_far = so_far + sizes_ref[cluster]
+
+    def cluster_of(ids):
+        return sum((ids >= start).astype(jnp.int32) for start in starts)
+
+    row_ids = lax.broadcasted_iota(jnp.int32, (query_rows, 1), 0)
+    query_cluster = cluster_of(group * slots + row_ids // rows)
+    lane_ids = lax.broadcasted_iota(jnp.int32, (1, slots * slice_rows), 1)
+    lane_block = lane_ids // slice_rows
+    lane_row = lane_ids % slice_rows + (half * 2 + core) * slice_rows
+
+    top[...] = jnp.full_like(top, negative)
+    mass[...] = jnp.zeros_like(mass)
+    total[...] = jnp.zeros_like(total)
+    share_in.wait_recv()
+    keys[zero_slot] = queries[:, key_rows(core), :].reshape(keys.shape[1:])
+
+    def step(turn, carry):
+        far = jnp.where(turn == 2, 2, jnp.where(turn == 3, -2, 0))
+        near = jnp.where(turn == 1, 1, jnp.where(turn == 4, -1, 0))
+        last = jnp.where(turn == 5, 3, jnp.where(turn == 6, -3, 0))
+        offset = toward * (far + near + last)
+
+        @pl.when(turn == 1)
+        def _():
+            for part in range(2):
+                arrived(toward, part)
+
+                @pl.when(has_behind)
+                def _():
+                    relay_behind(part).start()
+
+            @pl.when(has_ahead)
+            def _():
+                for part in range(2):
+                    arrived(2 * toward, part)
+                    relay_across(part).start()
+
+        @pl.when((turn == 3) & has_behind)
+        def _():
+            for part in range(2):
+                arrived(-2 * toward, part)
+
+        @pl.when((turn == 4) & has_behind)
+        def _():
+            for part in range(2):
+                arrived(-toward, part)
+
+                @pl.when(has_ahead)
+                def _():
+                    relay_ahead(part).start()
+
+        @pl.when((turn == 5) & has_ahead)
+        def _():
+            for part in range(2):
+                arrived(3 * toward, part)
+
+        @pl.when((turn == 6) & has_behind2)
+        def _():
+            for part in range(2):
+                arrived(-3 * toward, part)
+
+        present = (group + offset >= 0) & (group + offset < groups)
+
+        @pl.when(present)
+        def _():
+            first_block = (group + offset) * slots
+            valid = jnp.zeros_like(lane_ids)
+            for local in range(slots):
+                valid = jnp.where(lane_block == local, counts_ref[first_block + local], valid)
+            key_cluster = jnp.where(lane_row < valid, cluster_of(first_block + lane_block), -1)
+            self_row = jnp.where(offset == 0, lane_block * rows + lane_row, -1)
+            block_keys = keys[zero_slot + offset].reshape(slots * slice_rows, width)
+            scores = sharpness * lax.dot_general(
+                queries[...].reshape(query_rows, width), block_keys,
+                (((1,), (1,)), ((), ())), preferred_element_type=jnp.float32,
+            )
+            kept = (query_cluster == key_cluster) & (row_ids != self_row)
+            scores = jnp.where(kept, scores, 2.0 * negative)
+            new_top = jnp.maximum(top[...], jnp.max(scores, axis=1, keepdims=True))
+            scale = jnp.exp(top[...] - new_top)
+            weight = jnp.exp(scores - new_top)
+            top[...] = new_top
+            mass[...] = mass[...] * scale + jnp.sum(weight, axis=1, keepdims=True)
+            weight = weight.astype(jnp.bfloat16)
+            piece = min(256, width)
+            for column in range(0, width, piece):
+                total[:, column:column + piece] = total[:, column:column + piece] * scale + jnp.dot(
+                    weight, block_keys[:, column:column + piece], preferred_element_type=jnp.float32
+                )
+
+        return carry
+
+    lax.fori_loop(0, 7, step, 0)
+
+    eye = (
+        lax.broadcasted_iota(jnp.int32, (half_rows, half_rows), 0)
+        == lax.broadcasted_iota(jnp.int32, (half_rows, half_rows), 1)
+    )
+
+    def to_lanes(column):
+        return jnp.sum(jnp.where(eye, column, 0.0), axis=0, keepdims=True)
+
+    def to_rows(lanes):
+        return jnp.sum(jnp.where(eye, lanes, 0.0), axis=1, keepdims=True)
+
+    def rows_of(block, side):
+        return pl.ds(pl.multiple_of(block * rows + side * half_rows, half_rows), half_rows)
+
+    def chip_copy(piece):
+        return (
+            pltpu.make_async_remote_copy(
+                src_ref=chip_stats_out.at[piece], dst_ref=chip_stats_in.at[piece],
+                send_sem=chip_stats_send.at[piece], recv_sem=chip_stats_recv.at[piece],
+                device_id=device(group, 1 - core), device_id_type=MESH,
+            ),
+            pltpu.make_async_remote_copy(
+                src_ref=chip_out.at[piece], dst_ref=chip_in.at[piece],
+                send_sem=chip_send.at[piece], recv_sem=chip_recv.at[piece],
+                device_id=device(group, 1 - core), device_id_type=MESH,
+            ),
+        )
+
+    def pair_copy(local):
+        return (
+            pltpu.make_async_remote_copy(
+                src_ref=pair_stats_out.at[local], dst_ref=pair_stats_in.at[local],
+                send_sem=pair_stats_send.at[local], recv_sem=pair_stats_recv.at[local],
+                device_id=partner, device_id_type=MESH,
+            ),
+            pltpu.make_async_remote_copy(
+                src_ref=pair_out.at[local], dst_ref=pair_in.at[local],
+                send_sem=pair_send.at[local], recv_sem=pair_recv.at[local],
+                device_id=partner, device_id_type=MESH,
+            ),
+        )
+
+    pieces = [(remote, local) for remote in range(2) for local in range(blocks)]
+
+    def side_of(remote):
+        return 1 - half if remote == 0 else half
+
+    for index, (remote, local) in enumerate(pieces):
+        span = rows_of((1 - core) * blocks + local, side_of(remote))
+        chip_out[index] = total[span].astype(jnp.bfloat16)
+        chip_stats_out[index, 0:1, :half_rows] = to_lanes(top[span])
+        chip_stats_out[index, 1:2, :half_rows] = to_lanes(mass[span])
+        for copy in chip_copy(index):
+            copy.start()
+
+    for index, (remote, local) in enumerate(pieces):
+        for copy in chip_copy(index):
+            copy.wait_recv()
+        span = rows_of(core * blocks + local, side_of(remote))
+        other_top = to_rows(chip_stats_in[index, 0:1, :half_rows])
+        other_mass = to_rows(chip_stats_in[index, 1:2, :half_rows])
+        new_top = jnp.maximum(top[span], other_top)
+        scale = jnp.exp(top[span] - new_top)
+        other_scale = jnp.exp(other_top - new_top)
+        new_mass = mass[span] * scale + other_mass * other_scale
+        new_total = total[span] * scale + chip_in[index].astype(jnp.float32) * other_scale
+        if remote == 0:
+            pair_out[local] = new_total.astype(jnp.bfloat16)
+            pair_stats_out[local, 0:1, :half_rows] = to_lanes(new_top)
+            pair_stats_out[local, 1:2, :half_rows] = to_lanes(new_mass)
+            for copy in pair_copy(local):
+                copy.start()
+        else:
+            total[span] = new_total
+            top[span] = new_top
+            mass[span] = new_mass
+
+    place = lax.broadcasted_iota(jnp.int32, (half_rows, 1), 0) + half * half_rows
+    for local in range(blocks):
+        for copy in pair_copy(local):
+            copy.wait_recv()
+        span = rows_of(core * blocks + local, half)
+        other_top = to_rows(pair_stats_in[local, 0:1, :half_rows])
+        other_mass = to_rows(pair_stats_in[local, 1:2, :half_rows])
+        new_top = jnp.maximum(top[span], other_top)
+        scale = jnp.exp(top[span] - new_top)
+        other_scale = jnp.exp(other_top - new_top)
+        new_mass = mass[span] * scale + other_mass * other_scale
+        row_valid = place < counts_ref[mine * blocks + local]
+        own_part = total[span] * (scale / new_mass)
+        other_part = pair_in[local].astype(jnp.float32) * (other_scale / new_mass)
+        near_ref[local] = jnp.where(row_valid, own_part + other_part, 0.0).astype(jnp.bfloat16)
+        logs = jnp.where(row_valid, new_top + jnp.log(new_mass), 0.0)
+        mass_ref[local:local + 1, :] = to_lanes(logs)
+
+    share.wait_send()
+    for other_core in range(2):
+        direct_across(other_core).wait_send()
+
+        @pl.when(has_ahead)
+        def _():
+            direct_ahead(other_core).wait_send()
+            relay_across(other_core).wait_send()
+
+        @pl.when(has_behind)
+        def _():
+            direct_behind(other_core).wait_send()
+            relay_behind(other_core).wait_send()
+
+        @pl.when(has_ahead & has_behind)
+        def _():
+            relay_ahead(other_core).wait_send()
+
+    for index in range(len(pieces)):
+        for copy in chip_copy(index):
+            copy.wait_send()
+    for local in range(blocks):
+        for copy in pair_copy(local):
+            copy.wait_send()
+
+
+def kernel_body(embeddings, cluster_sizes, row_counts):
+    blocks, rows, width = embeddings.shape
+    groups = lax.axis_size("own") // 2
+    slots, slice_rows, half_rows = 2 * blocks, rows // 4, rows // 2
+    query_rows = slots * rows
+    wide, narrow = jnp.float32, jnp.bfloat16
+    stats = (8, 128)
+    dma = pltpu.SemaphoreType.DMA
+    smem, vmem = pl.BlockSpec(memory_space=pltpu.SMEM), pl.BlockSpec(memory_space=pltpu.VMEM)
+    return pl.pallas_call(
+        functools.partial(kernel, groups, blocks, rows, slice_rows),
+        out_shape=(
+            jax.ShapeDtypeStruct((blocks, half_rows, width), narrow),
+            jax.ShapeDtypeStruct((blocks, half_rows), wide),
+        ),
+        in_specs=[smem, smem, vmem],
+        out_specs=(vmem, vmem),
+        scratch_shapes=[
+            pltpu.VMEM((slots, rows, width), narrow),
+            pltpu.VMEM((7, 2, blocks, slice_rows, width), narrow),
+            pltpu.VMEM((query_rows, 1), wide),
+            pltpu.VMEM((query_rows, 1), wide),
+            pltpu.VMEM((query_rows, width), wide),
+            pltpu.VMEM((2 * blocks, half_rows, width), narrow),
+            pltpu.VMEM((2 * blocks, half_rows, width), narrow),
+            pltpu.VMEM((2 * blocks, *stats), wide),
+            pltpu.VMEM((2 * blocks, *stats), wide),
+            pltpu.VMEM((blocks, half_rows, width), narrow),
+            pltpu.VMEM((blocks, half_rows, width), narrow),
+            pltpu.VMEM((blocks, *stats), wide),
+            pltpu.VMEM((blocks, *stats), wide),
+            dma((1,)), dma((1,)),
+            dma((3, 2)), dma((7, 2)), dma((3, 2)),
+            dma((2 * blocks,)), dma((2 * blocks,)), dma((2 * blocks,)), dma((2 * blocks,)),
+            dma((blocks,)), dma((blocks,)), dma((blocks,)), dma((blocks,)),
+        ],
+        compiler_params=pltpu.CompilerParams(
+            collective_id=0, has_side_effects=True, vmem_limit_bytes=40 * 1024 * 1024
+        ),
+        cost_estimate=pl.CostEstimate(
+            flops=4 * query_rows * 7 * slots * slice_rows * width,
+            bytes_accessed=embeddings.size * 4,
+            transcendentals=query_rows * 7 * slots * slice_rows,
+        ),
+    )(cluster_sizes, row_counts, embeddings)
+
+
+def fits_kernel(block_shape):
+    blocks, rows, width = block_shape
+    covered = (SPAN + 2 * blocks - 2) // (2 * blocks) <= 3
+    whole_tiles = rows % 128 == 0 and width % 128 == 0
+    return lax.axis_size("pair") == 2 and lax.axis_size("own") % 4 == 0 and covered and whole_tiles
+
+
+def device_part(embeddings, cluster_sizes, row_counts):
+    chosen = kernel_body if fits_kernel(embeddings.shape) else body
+    return chosen(embeddings, cluster_sizes, row_counts)
+
+
 def solution(mesh):
     placed = (P("own", None, None), P(), P())
     return jax.shard_map(
-        body,
+        device_part,
         mesh=mesh,
         in_specs=placed,
         out_specs=(P("own", "pair", None), P("own", "pair")),

time: 336 us -> 36.9 us (0.11)
  the two profiles are of different devices: /device:TPU:6 before, /device:TPU:2 now
where the time goes in v1:
time: 36.9 us; the launch traced here: 36.7 us
  Pallas kernels  32.3 us (88%)
  local copies, waits for them, and re-layouts  3.79 us (10%)
  between operations  0.65 us (2%)
    pallas_call x1, Pallas kernels, kernel_body(): pl.pallas_call(functools.partial(kernel, groups, blocks, rows, slice_rows...  32.3 us
    unnamed x8, local copies, waits for them, and re-layouts  3.79 us

profile of v1, /device:TPU:2, one launch (start us, length us, event | category | flops | bytes accessed | tf_op | source)
XLA Modules:
  0.0 36.7 jit_solution(5086185440476592114)
XLA Ops:
  0.6 0.0 copy-start
  0.6 1.2 %copy-done = f32[2,128,1024]{2,1,0:T(8,128)S(1)} copy-done((f32[2,128,1024]{2,1,0:T(8,128)S(1)}, f32[2,128,1024]{2,1,0:T(8,128)}, u32[]{:S(2)}) %copy-start) | copy-done | bytes 1048600
  1.9 0.0 copy-start.1
  1.9 0.7 %copy-done.1 = s32[8]{0:T(128)S(1)} copy-done((s32[8]{0:T(128)S(1)}, s32[8]{0:T(128)}, u32[]{:S(2)}) %copy-start.1) | copy-done | bytes 56
  2.5 0.0 copy-start.2
  2.5 0.7 %copy-done.2 = s32[32]{0:T(128)S(1)} copy-done((s32[32]{0:T(128)S(1)}, s32[32]{0:T(128)}, u32[]{:S(2)}) %copy-start.2) | copy-done | bytes 152
  3.2 32.3 %shard_map.50 = (bf16[2,64,1024]{2,1,0:T(8,128)(2,1)S(1)}, f32[2,64]{1,0:T(2,128)S(1)}) custom-call(s32[8]{0:T(128)S(1)} %copy-done.1, s32[32]{0:T(128)S(1)} %copy-done.2, f32[2,128,1024]{2,1,0:T(8,128)S(1)} %copy-done), custom_call_target="tpu_custom_call" | custom-call | flops 1879048192 | bytes 1048576 | tf_op jit(solution)/shard_map/pallas_call | solution.py:574
  35.5 0.7 %copy.7 = bf16[2,64,1024]{2,1,0:T(8,128)(2,1)} copy(bf16[2,64,1024]{2,1,0:T(8,128)(2,1)S(1)} %get-tuple-element.4) | data formatting | bytes 524288
  36.2 0.6 %copy.8 = f32[2,64]{1,0:T(2,128)} copy(f32[2,64]{1,0:T(2,128)S(1)} %get-tuple-element.5) | data formatting | bytes 1024
Async XLA Ops:
  0.6 1.2 %copy-start = (f32[2,128,1024]{2,1,0:T(8,128)S(1)}, f32[2,128,1024]{2,1,0:T(8,128)}, u32[]{:S(2)}) copy-start(f32[2,128,1024]{2,1,0:T(8,128)} %emb_ref.1) | copy-start | bytes 3145732
  1.9 0.7 %copy-start.1 = (s32[8]{0:T(128)S(1)}, s32[8]{0:T(128)}, u32[]{:S(2)}) copy-start(s32[8]{0:T(128)} %sizes_ref.1) | copy-start | bytes 100
  2.5 0.7 %copy-start.2 = (s32[32]{0:T(128)S(1)}, s32[32]{0:T(128)}, u32[]{:S(2)}) copy-start(s32[32]{0:T(128)} %counts_ref.1) | copy-start | bytes 388

commit v2 on v0

--- a/solution.py
+++ b/solution.py
@@ -1,6 +1,10 @@
+import functools
+
 import jax
 import jax.numpy as jnp
 from jax import lax
+from jax.experimental import pallas as pl
+from jax.experimental.pallas import tpu as pltpu
 from jax.sharding import PartitionSpec as P
 
 SPAN = 12
@@ -190,10 +194,501 @@
     return (near_sums, log_masses)
 
 
+MESH = pl.DeviceIdType.MESH
+
+
+def kernel(
+    groups, blocks, rows, slice_rows, block_total,
+    sizes_hbm, counts_hbm, emb_hbm, near_ref, mass_ref,
+    sizes_ref, counts_ref, emb_ref, queries, keys, top, mass, total,
+    chip_out, chip_in, chip_stats_out, chip_stats_in,
+    pair_out, pair_in, pair_stats_out, pair_stats_in,
+    load, share_send, share_recv, direct_send, key_recv, relay_send,
+    chip_send, chip_recv, pair_send, pair_recv,
+):
+    width = emb_ref.shape[2]
+    mine = lax.axis_index("own")
+    half = lax.axis_index("pair")
+    group, core = mine // 2, mine % 2
+    toward = 1 - 2 * (group % 2)
+    across = group + toward
+    ahead, behind = group + 2 * toward, group - 2 * toward
+    has_ahead = (ahead >= 0) & (ahead < groups)
+    has_behind = (behind >= 0) & (behind < groups)
+    behind2 = group - 4 * toward
+    has_behind2 = (behind2 >= 0) & (behind2 < groups)
+    slots = 2 * blocks
+    half_rows = rows // 2
+    core_rows = blocks * rows
+    slot_keys = slots * slice_rows
+
+    def device(group_index, core_index):
+        return (group_index * 2 + core_index, half)
+
+    partner = (mine, 1 - half)
+    sibling = device(group, 1 - core)
+
+    def half_span(side):
+        return pl.ds(pl.multiple_of(side * half_rows, half_rows), half_rows)
+
+    def load_rows(index, side):
+        return pltpu.make_async_copy(
+            emb_hbm.at[:, half_span(side)], emb_ref.at[:, half_span(side)], load.at[index]
+        )
+
+    load_rows(0, half).start()
+    load_rows(1, 1 - half).start()
+    load_sizes = pltpu.make_async_copy(sizes_hbm, sizes_ref, load.at[2])
+    load_counts = pltpu.make_async_copy(counts_hbm, counts_ref, load.at[3])
+    load_sizes.start()
+    load_counts.start()
+
+    barrier = pltpu.get_barrier_semaphore()
+
+    def greet(target):
+        pl.semaphore_signal(barrier, inc=1, device_id=target, device_id_type=MESH)
+
+    greet(sibling)
+    greet(partner)
+    for other_core in range(2):
+        greet(device(across, other_core))
+
+    @pl.when(has_ahead)
+    def _():
+        for other_core in range(2):
+            greet(device(ahead, other_core))
+
+    @pl.when(has_behind)
+    def _():
+        for other_core in range(2):
+            greet(device(behind, other_core))
+
+    def normalise(side):
+        for local in range(blocks):
+            values = emb_ref[local, half_span(side), :]
+            squares = jnp.sum(values * values, axis=-1, keepdims=True)
+            queries[core * blocks + local, half_span(side), :] = (
+                values * lax.rsqrt(squares + 1e-06)
+            ).astype(jnp.bfloat16)
+
+    load_rows(0, half).wait()
+    normalise(half)
+
+    own_blocks = pl.ds(core * blocks, blocks)
+    other_blocks = pl.ds((1 - core) * blocks, blocks)
+
+    def key_rows(core_index):
+        return pl.ds(pl.multiple_of((half * 2 + core_index) * slice_rows, slice_rows), slice_rows)
+
+    def share(index, side):
+        return pltpu.make_async_remote_copy(
+            src_ref=queries.at[own_blocks, half_span(side)],
+            dst_ref=queries.at[own_blocks, half_span(side)],
+            send_sem=share_send.at[index],
+            recv_sem=share_recv.at[index],
+            device_id=sibling,
+            device_id_type=MESH,
+        )
+
+    def share_in(index, side):
+        return pltpu.make_async_remote_copy(
+            src_ref=queries.at[other_blocks, half_span(side)],
+            dst_ref=queries.at[other_blocks, half_span(side)],
+            send_sem=share_send.at[index],
+            recv_sem=share_recv.at[index],
+            device_id=sibling,
+            device_id_type=MESH,
+        )
+
+    def direct(place, target, slot, other_core):
+        return pltpu.make_async_remote_copy(
+            src_ref=queries.at[own_blocks, key_rows(other_core)],
+            dst_ref=keys.at[slot, core],
+            send_sem=direct_send.at[place, other_core],
+            recv_sem=key_recv.at[slot, core],
+            device_id=device(target, other_core),
+            device_id_type=MESH,
+        )
+
+    def relay(place, source, target, slot, part):
+        return pltpu.make_async_remote_copy(
+            src_ref=keys.at[source, part],
+            dst_ref=keys.at[slot, part],
+            send_sem=relay_send.at[place, part],
+            recv_sem=key_recv.at[slot, part],
+            device_id=device(target, core),
+            device_id_type=MESH,
+        )
+
+    def arrived(slot, part):
+        relay(0, slot, across, slot, part).wait_recv()
+
+    def direct_across(other_core):
+        return direct(0, across, 1, other_core)
+
+    def direct_ahead(other_core):
+        return direct(1, ahead, 3, other_core)
+
+    def direct_behind(other_core):
+        return direct(2, behind, 2, other_core)
+
+    def relay_across(part):
+        return relay(0, 2, across, 4, part)
+
+    def relay_behind(part):
+        return relay(1, 1, behind, 5, part)
+
+    def relay_ahead(part):
+        return relay(2, 4, ahead, 6, part)
+
+    neighbours = 4 + 2 * has_ahead.astype(jnp.int32) + 2 * has_behind.astype(jnp.int32)
+    pl.semaphore_wait(barrier, neighbours)
+
+    for other_core in range(2):
+        direct_across(other_core).start()
+
+        @pl.when(has_behind)
+        def _():
+            direct_behind(other_core).start()
+
+        @pl.when(has_ahead)
+        def _():
+            direct_ahead(other_core).start()
+
+    share(0, half).start()
+    load_rows(1, 1 - half).wait()
+    normalise(1 - half)
+    share(1, 1 - half).start()
+    load_sizes.wait()
+    load_counts.wait()
+
+    starts = []
+    so_far = jnp.int32(0)
+    for cluster in range(sizes_ref.shape[0]):
+        starts.append(so_far)
+        so_far = so_far + sizes_ref[cluster]
+
+    def cluster_of(ids):
+        return sum((ids >= start).astype(jnp.int32) for start in starts)
+
+    top[...] = jnp.full_like(top, negative)
+    mass[...] = jnp.zeros_like(mass)
+    total[...] = jnp.zeros_like(total)
+
+    @pl.when(jnp.logical_not(has_ahead))
+    def _():
+        keys[2] = jnp.zeros_like(keys[2])
+        keys[5] = jnp.zeros_like(keys[5])
+
+    @pl.when(jnp.logical_not(has_behind))
+    def _():
+        keys[3] = jnp.zeros_like(keys[3])
+        keys[4] = jnp.zeros_like(keys[4])
+
+    @pl.when(jnp.logical_not(has_behind2))
+    def _():
+        keys[6] = jnp.zeros_like(keys[6])
+
+    def fold(first_slot, distances, side_core):
+        taken = len(distances)
+        lane_ids = lax.broadcasted_iota(jnp.int32, (1, taken * slot_keys), 1)
+        lane_local = lane_ids % slot_keys
+        lane_row = lane_local % slice_rows + (half * 2 + core) * slice_rows
+        lane_block = jnp.zeros_like(lane_ids)
+        valid = jnp.zeros_like(lane_ids)
+        for index, distance in enumerate(distances):
+            first_block = (group + toward * distance) * slots
+            for local in range(slots):
+                block = first_block + local
+                there = lane_ids // slice_rows == index * slots + local
+                inside = (block >= 0) & (block < block_total)
+                count = counts_ref[jnp.clip(block, 0, block_total - 1)]
+                valid = jnp.where(there, jnp.where(inside, count, 0), valid)
+                lane_block = jnp.where(there, block, lane_block)
+        key_cluster = jnp.where(lane_row < valid, cluster_of(lane_block), -1)
+        row_ids = lax.broadcasted_iota(jnp.int32, (core_rows, 1), 0) + (
+            (group * 2 + side_core) * core_rows
+        )
+        query_cluster = cluster_of(row_ids // rows)
+        block_keys = keys[first_slot:first_slot + taken] if isinstance(first_slot, int) else (
+            keys[pl.ds(first_slot, taken)]
+        )
+        block_keys = block_keys.reshape(taken * slot_keys, width)
+        side_blocks = pl.ds(side_core * blocks, blocks)
+        span = pl.ds(pl.multiple_of(side_core * core_rows, core_rows), core_rows)
+        scores = sharpness * lax.dot_general(
+            queries[side_blocks].reshape(core_rows, width), block_keys,
+            (((1,), (1,)), ((), ())), preferred_element_type=jnp.float32,
+        )
+        kept = query_cluster == key_cluster
+        if taken == 1:
+            kept = kept & (row_ids != lane_block * rows + lane_row)
+        scores = jnp.where(kept, scores, 2.0 * negative)
+        old_top = top[span]
+        new_top = jnp.maximum(old_top, jnp.max(scores, axis=1, keepdims=True))
+        scale = jnp.exp(old_top - new_top)
+        weight = jnp.exp(scores - new_top)
+        top[span] = new_top
+        mass[span] = mass[span] * scale + jnp.sum(weight, axis=1, keepdims=True)
+        weight = weight.astype(jnp.bfloat16)
+        piece = min(256, width)
+        for column in range(0, width, piece):
+            columns = slice(column, column + piece)
+            total[span, columns] = total[span, columns] * scale + jnp.dot(
+                weight, block_keys[:, columns], preferred_element_type=jnp.float32
+            )
+
+    share_in(0, half).wait_recv()
+    keys[0] = queries[:, key_rows(core), :].reshape(keys.shape[1:])
+    share_in(1, 1 - half).wait_recv()
+
+    def own_fold(side_core, carry):
+        fold(0, (0,), side_core)
+        return carry
+
+    lax.fori_loop(0, 2, own_fold, 0)
+
+    def pair_fold(turn, carry):
+        @pl.when(turn == 0)
+        def _():
+            for part in range(2):
+                arrived(1, part)
+
+                @pl.when(has_behind)
+                def _():
+                    relay_behind(part).start()
+
+            @pl.when(has_ahead)
+            def _():
+                for part in range(2):
+                    arrived(2, part)
+                    relay_across(part).start()
+
+        @pl.when((turn == 2) & has_behind)
+        def _():
+            for part in range(2):
+                arrived(4, part)
+
+                @pl.when(has_ahead)
+                def _():
+                    relay_ahead(part).start()
+
+            for part in range(2):
+                arrived(3, part)
+
+        late = turn // 2
+        fold(1 + 2 * late, (1 - 3 * late, 2 - 3 * late), turn % 2)
+        return carry
+
+    lax.fori_loop(0, 4, pair_fold, 0)
+
+    eye = (
+        lax.broadcasted_iota(jnp.int32, (half_rows, half_rows), 0)
+        == lax.broadcasted_iota(jnp.int32, (half_rows, half_rows), 1)
+    )
+
+    def to_lanes(column):
+        return jnp.sum(jnp.where(eye, column, 0.0), axis=0, keepdims=True)
+
+    def to_rows(lanes):
+        return jnp.sum(jnp.where(eye, lanes, 0.0), axis=1, keepdims=True)
+
+    def rows_of(block, side):
+        return pl.ds(pl.multiple_of(block * rows + side * half_rows, half_rows), half_rows)
+
+    def sent(source, target, send, recv, index, destination):
+        return pltpu.make_async_remote_copy(
+            src_ref=source, dst_ref=target, send_sem=send.at[index], recv_sem=recv.at[index],
+            device_id=destination, device_id_type=MESH,
+        )
+
+    def chip_copy(remote):
+        return sent(chip_out.at[remote], chip_in.at[remote], chip_send, chip_recv, remote, sibling)
+
+    def pair_copy(local):
+        return sent(pair_out.at[local], pair_in.at[local], pair_send, pair_recv, local, partner)
+
+    chip_stats = sent(chip_stats_out, chip_stats_in, chip_send, chip_recv, 2, sibling)
+    pair_stats = sent(pair_stats_out, pair_stats_in, pair_send, pair_recv, blocks, partner)
+    sides = (1 - half, half)
+
+    @pl.when(has_ahead)
+    def _():
+        for part in range(2):
+            arrived(5, part)
+
+    @pl.when(has_behind2)
+    def _():
+        for part in range(2):
+            arrived(6, part)
+
+    def last_fold(turn, carry):
+        fold(5, (3, -3), jnp.where(turn == 0, 1 - core, core))
+
+        @pl.when(turn == 0)
+        def _():
+            for remote in range(2):
+                for local in range(blocks):
+                    span = rows_of((1 - core) * blocks + local, sides[remote])
+                    place = remote * blocks + local
+                    chip_stats_out[place, 0:1, :half_rows] = to_lanes(top[span])
+                    chip_stats_out[place, 1:2, :half_rows] = to_lanes(mass[span])
+            chip_stats.start()
+            for remote in range(2):
+                for local in range(blocks):
+                    span = rows_of((1 - core) * blocks + local, sides[remote])
+                    chip_out[remote, local] = total[span].astype(jnp.bfloat16)
+                chip_copy(remote).start()
+
+        return carry
+
+    lax.fori_loop(0, 2, last_fold, 0)
+
+    chip_stats.wait_recv()
+    scales = {}
+    for remote in range(2):
+        for local in range(blocks):
+            span = rows_of(core * blocks + local, sides[remote])
+            place = remote * blocks + local
+            other_top = to_rows(chip_stats_in[place, 0:1, :half_rows])
+            other_mass = to_rows(chip_stats_in[place, 1:2, :half_rows])
+            new_top = jnp.maximum(top[span], other_top)
+            scale = jnp.exp(top[span] - new_top)
+            other_scale = jnp.exp(other_top - new_top)
+            new_mass = mass[span] * scale + other_mass * other_scale
+            scales[remote, local] = (scale, other_scale, new_top, new_mass)
+            if remote == 0:
+                pair_stats_out[local, 0:1, :half_rows] = to_lanes(new_top)
+                pair_stats_out[local, 1:2, :half_rows] = to_lanes(new_mass)
+    pair_stats.start()
+    for remote in range(2):
+        chip_copy(remote).wait_recv()
+        for local in range(blocks):
+            span = rows_of(core * blocks + local, sides[remote])
+            scale, other_scale, new_top, new_mass = scales[remote, local]
+            new_total = total[span] * scale + chip_in[remote, local].astype(jnp.float32) * other_scale
+            if remote == 0:
+                pair_out[local] = new_total.astype(jnp.bfloat16)
+                pair_copy(local).start()
+            else:
+                total[span] = new_total
+
+    place = lax.broadcasted_iota(jnp.int32, (half_rows, 1), 0) + half * half_rows
+    pair_stats.wait_recv()
+    final = []
+    for local in range(blocks):
+        other_top = to_rows(pair_stats_in[local, 0:1, :half_rows])
+        other_mass = to_rows(pair_stats_in[local, 1:2, :half_rows])
+        _, _, own_top, own_mass = scales[1, local]
+        new_top = jnp.maximum(own_top, other_top)
+        scale = jnp.exp(own_top - new_top)
+        other_scale = jnp.exp(other_top - new_top)
+        new_mass = own_mass * scale + other_mass * other_scale
+        row_valid = place < counts_ref[mine * blocks + local]
+        final.append((scale / new_mass, other_scale / new_mass, row_valid))
+        logs = jnp.where(row_valid, new_top + jnp.log(new_mass), 0.0)
+        mass_ref[local:local + 1, :] = to_lanes(logs)
+
+    share(0, half).wait_send()
+    share(1, 1 - half).wait_send()
+    for other_core in range(2):
+        direct_across(other_core).wait_send()
+
+        @pl.when(has_ahead)
+        def _():
+            direct_ahead(other_core).wait_send()
+            relay_across(other_core).wait_send()
+
+        @pl.when(has_behind)
+        def _():
+            direct_behind(other_core).wait_send()
+            relay_behind(other_core).wait_send()
+
+        @pl.when(has_ahead & has_behind)
+        def _():
+            relay_ahead(other_core).wait_send()
+
+    chip_stats.wait_send()
+    pair_stats.wait_send()
+    for remote in range(2):
+        chip_copy(remote).wait_send()
+
+    for local in range(blocks):
+        pair_copy(local).wait_recv()
+        span = rows_of(core * blocks + local, half)
+        scale, other_scale, row_valid = final[local]
+        merged = total[span] * scale + pair_in[local].astype(jnp.float32) * other_scale
+        near_ref[local] = jnp.where(row_valid, merged, 0.0).astype(jnp.bfloat16)
+
+    for local in range(blocks):
+        pair_copy(local).wait_send()
+
+
+def kernel_body(embeddings, cluster_sizes, row_counts):
+    blocks, rows, width = embeddings.shape
+    groups = lax.axis_size("own") // 2
+    slots, slice_rows, half_rows = 2 * blocks, rows // 4, rows // 2
+    query_rows = slots * rows
+    wide, narrow = jnp.float32, jnp.bfloat16
+    stats = (8, 128)
+    dma = pltpu.SemaphoreType.DMA
+    hbm, vmem = pl.BlockSpec(memory_space=pltpu.HBM), pl.BlockSpec(memory_space=pltpu.VMEM)
+    return pl.pallas_call(
+        functools.partial(kernel, groups, blocks, rows, slice_rows, row_counts.shape[0]),
+        out_shape=(
+            jax.ShapeDtypeStruct((blocks, half_rows, width), narrow),
+            jax.ShapeDtypeStruct((blocks, half_rows), wide),
+        ),
+        in_specs=[hbm, hbm, hbm],
+        out_specs=(vmem, vmem),
+        scratch_shapes=[
+            pltpu.SMEM(cluster_sizes.shape, jnp.int32),
+            pltpu.SMEM(row_counts.shape, jnp.int32),
+            pltpu.VMEM(embeddings.shape, wide),
+            pltpu.VMEM((slots, rows, width), narrow),
+            pltpu.VMEM((7, 2, blocks, slice_rows, width), narrow),
+            pltpu.VMEM((query_rows, 1), wide),
+            pltpu.VMEM((query_rows, 1), wide),
+            pltpu.VMEM((query_rows, width), wide),
+            pltpu.VMEM((2, blocks, half_rows, width), narrow),
+            pltpu.VMEM((2, blocks, half_rows, width), narrow),
+            pltpu.VMEM((2 * blocks, *stats), wide),
+            pltpu.VMEM((2 * blocks, *stats), wide),
+            pltpu.VMEM((blocks, half_rows, width), narrow),
+            pltpu.VMEM((blocks, half_rows, width), narrow),
+            pltpu.VMEM((blocks, *stats), wide),
+            pltpu.VMEM((blocks, *stats), wide),
+            dma((4,)), dma((2,)), dma((2,)),
+            dma((3, 2)), dma((7, 2)), dma((3, 2)),
+            dma((3,)), dma((3,)), dma((blocks + 1,)), dma((blocks + 1,)),
+        ],
+        compiler_params=pltpu.CompilerParams(
+            collective_id=0, has_side_effects=True, vmem_limit_bytes=56 * 1024 * 1024
+        ),
+        cost_estimate=pl.CostEstimate(
+            flops=4 * query_rows * 7 * slots * slice_rows * width,
+            bytes_accessed=embeddings.size * 4,
+            transcendentals=query_rows * 7 * slots * slice_rows,
+        ),
+    )(cluster_sizes, row_counts, embeddings)
+
+
+def fits_kernel(block_shape):
+    blocks, rows, width = block_shape
+    covered = (SPAN + 2 * blocks - 2) // (2 * blocks) <= 3
+    whole_tiles = rows % 128 == 0 and width % 128 == 0
+    return lax.axis_size("pair") == 2 and lax.axis_size("own") % 4 == 0 and covered and whole_tiles
+
+
+def device_part(embeddings, cluster_sizes, row_counts):
+    chosen = kernel_body if fits_kernel(embeddings.shape) else body
+    return chosen(embeddings, cluster_sizes, row_counts)
+
+
 def solution(mesh):
     placed = (P("own", None, None), P(), P())
     return jax.shard_map(
-        body,
+        device_part,
         mesh=mesh,
         in_specs=placed,
         out_specs=(P("own", "pair", None), P("own", "pair")),

time: 336 us -> 35.1 us (0.10)
  the two profiles are of different devices: /device:TPU:6 before, /device:TPU:10 now
where the time goes in v2:
time: 35.1 us; the launch traced here: 35 us
  Pallas kernels  32.1 us (91%)
  local copies, waits for them, and re-layouts  2.24 us (6%)
  between operations  0.65 us (2%)
    pallas_call x1, Pallas kernels, kernel_body(): pl.pallas_call(functools.partial(kernel, groups, blocks, rows, slice_rows...  32.1 us
    unnamed x4, local copies, waits for them, and re-layouts  2.24 us

profile of v2, /device:TPU:10, one launch (start us, length us, event | category | flops | bytes accessed | tf_op | source)
XLA Modules:
  0.0 35.0 jit_solution(14008828316701678577)
XLA Ops:
  0.6 32.1 %shard_map.50 = (bf16[2,64,1024]{2,1,0:T(8,128)(2,1)}, f32[2,64]{1,0:T(2,128)}) custom-call(s32[8]{0:T(128)} %sizes_hbm.1, s32[32]{0:T(128)} %counts_hbm.1, f32[2,128,1024]{2,1,0:T(8,128)} %emb_hbm.1), custom_call_target="tpu_custom_call" | custom-call | flops 1879048192 | bytes 1048576 | tf_op jit(solution)/shard_map/pallas_call | solution.py:636
  32.7 0.0 copy-start
  32.7 1.7 %copy.7 = bf16[2,64,1024]{2,1,0:T(8,128)(2,1)} copy(bf16[2,64,1024]{2,1,0:T(8,128)(2,1)} %get-tuple-element.4) | data formatting | bytes 524288
  34.4 0.0 copy-done
  34.4 0.6 %copy.8 = f32[2,64]{1,0:T(2,128)} copy(f32[2,64]{1,0:T(2,128)S(1)} %copy-done) | data formatting | bytes 1024
Async XLA Ops:
  32.7 1.7 %copy-start = (f32[2,64]{1,0:T(2,128)S(1)}, f32[2,64]{1,0:T(2,128)}, u32[]{:S(2)}) copy-start(f32[2,64]{1,0:T(2,128)} %get-tuple-element.5) | copy-start | bytes 1540

commit v3 on v2

--- a/solution.py
+++ b/solution.py
@@ -300,60 +300,71 @@
             device_id_type=MESH,
         )
 
-    def direct(place, target, slot, other_core):
+    def direct(place, target, slot, other_core, local):
+        block = core * blocks + local
         return pltpu.make_async_remote_copy(
-            src_ref=queries.at[own_blocks, key_rows(other_core)],
-            dst_ref=keys.at[slot, core],
-            send_sem=direct_send.at[place, other_core],
-            recv_sem=key_recv.at[slot, core],
+            src_ref=queries.at[block, key_rows(other_core)],
+            dst_ref=keys.at[slot, block],
+            send_sem=direct_send.at[place, other_core, local],
+            recv_sem=key_recv.at[slot, block],
             device_id=device(target, other_core),
             device_id_type=MESH,
         )
 
-    def relay(place, source, target, slot, part):
+    def relay(place, source, target, slot, block):
         return pltpu.make_async_remote_copy(
-            src_ref=keys.at[source, part],
-            dst_ref=keys.at[slot, part],
-            send_sem=relay_send.at[place, part],
-            recv_sem=key_recv.at[slot, part],
+            src_ref=keys.at[source, block],
+            dst_ref=keys.at[slot, block],
+            send_sem=relay_send.at[place, block],
+            recv_sem=key_recv.at[slot, block],
             device_id=device(target, core),
             device_id_type=MESH,
         )
 
-    def arrived(slot, part):
-        relay(0, slot, across, slot, part).wait_recv()
-
-    def direct_across(other_core):
-        return direct(0, across, 1, other_core)
-
-    def direct_ahead(other_core):
-        return direct(1, ahead, 3, other_core)
-
-    def direct_behind(other_core):
-        return direct(2, behind, 2, other_core)
-
-    def relay_across(part):
-        return relay(0, 2, across, 4, part)
-
-    def relay_behind(part):
-        return relay(1, 1, behind, 5, part)
-
-    def relay_ahead(part):
-        return relay(2, 4, ahead, 6, part)
+    def arrived(slot, block):
+        relay(0, slot, across, slot, block).wait_recv()
+
+    def direct_across(other_core, local):
+        return direct(0, across, 1, other_core, local)
+
+    def direct_ahead(other_core, local):
+        return direct(1, ahead, 3, other_core, local)
+
+    def direct_behind(other_core, local):
+        return direct(2, behind, 2, other_core, local)
+
+    skip = (1 - toward) // 2
+    reach = slots - 1
+
+    def upper(index):
+        return index + 1 - skip
+
+    def lower(index):
+        return index + skip
+
+    def relay_across(index):
+        return relay(0, 2, across, 4, (index + skip) % slots)
+
+    def relay_behind(index):
+        return relay(1, 1, behind, 5, lower(index))
+
+    def relay_ahead(index):
+        return relay(2, 4, ahead, 6, upper(index))
 
     neighbours = 4 + 2 * has_ahead.astype(jnp.int32) + 2 * has_behind.astype(jnp.int32)
     pl.semaphore_wait(barrier, neighbours)
 
     for other_core in range(2):
-        direct_across(other_core).start()
-
-        @pl.when(has_behind)
-        def _():
-            direct_behind(other_core).start()
-
-        @pl.when(has_ahead)
-        def _():
-            direct_ahead(other_core).start()
+        for local in range(blocks):
+            direct_across(other_core, local).start()
+
+            @pl.when(has_behind)
+            def _():
+                direct_behind(other_core, local).start()
+
+            @pl.when(has_ahead)
+            def _():
+                direct_ahead(other_core, local).start()
 
     share(0, half).start()
     load_rows(1, 1 - half).wait()
@@ -385,9 +396,19 @@
         keys[3] = jnp.zeros_like(keys[3])
         keys[4] = jnp.zeros_like(keys[4])
 
+    @pl.when(has_ahead)
+    def _():
+        keys[5, lower(reach) % slots] = jnp.zeros_like(keys[5, 0])
+
+    @pl.when(has_behind2)
+    def _():
+        keys[6, upper(reach) % slots] = jnp.zeros_like(keys[6, 0])
+
     @pl.when(jnp.logical_not(has_behind2))
     def _():
         keys[6] = jnp.zeros_like(keys[6])
+
+    own_slot = 0
 
     def fold(first_slot, distances, side_core):
         taken = len(distances)
@@ -421,7 +442,7 @@
             (((1,), (1,)), ((), ())), preferred_element_type=jnp.float32,
         )
         kept = query_cluster == key_cluster
-        if taken == 1:
+        if first_slot is own_slot:
             kept = kept & (row_ids != lane_block * rows + lane_row)
         scores = jnp.where(kept, scores, 2.0 * negative)
         old_top = top[span]
@@ -439,11 +460,11 @@
             )
 
     share_in(0, half).wait_recv()
-    keys[0] = queries[:, key_rows(core), :].reshape(keys.shape[1:])
+    keys[0] = queries[:, key_rows(core), :]
     share_in(1, 1 - half).wait_recv()
 
     def own_fold(side_core, carry):
-        fold(0, (0,), side_core)
+        fold(own_slot, (0,), side_core)
         return carry
 
     lax.fori_loop(0, 2, own_fold, 0)
@@ -451,30 +472,33 @@
     def pair_fold(turn, carry):
         @pl.when(turn == 0)
         def _():
-            for part in range(2):
-                arrived(1, part)
+            @pl.when(has_ahead)
+            def _():
+                for index in range(slots):
+                    arrived(2, (index + skip) % slots)
+                    relay_across(index).start()
+
+            for index in range(reach):
+                arrived(1, lower(index))
 
                 @pl.when(has_behind)
                 def _():
-                    relay_behind(part).start()
-
-            @pl.when(has_ahead)
-            def _():
-                for part in range(2):
-                    arrived(2, part)
-                    relay_across(part).start()
+                    relay_behind(index).start()
+
+            arrived(1, lower(reach) % slots)
 
         @pl.when((turn == 2) & has_behind)
         def _():
-            for part in range(2):
-                arrived(4, part)
+            for index in range(reach):
+                arrived(4, upper(index))
 
                 @pl.when(has_ahead)
                 def _():
-                    relay_ahead(part).start()
-
-            for part in range(2):
-                arrived(3, part)
+                    relay_ahead(index).start()
+
+            arrived(4, upper(reach) % slots)
+            for block in range(slots):
+                arrived(3, block)
 
         late = turn // 2
         fold(1 + 2 * late, (1 - 3 * late, 2 - 3 * late), turn % 2)
@@ -514,16 +538,22 @@
 
     @pl.when(has_ahead)
     def _():
-        for part in range(2):
-            arrived(5, part)
+        for index in range(reach):
+            arrived(5, lower(index))
+
+    def late_fold(side_core, carry):
+        fold(5, (3,), side_core)
+        return carry
+
+    lax.fori_loop(0, 2, late_fold, 0)
 
     @pl.when(has_behind2)
     def _():
-        for part in range(2):
-            arrived(6, part)
+        for index in range(reach):
+            arrived(6, upper(index))
 
     def last_fold(turn, carry):
-        fold(5, (3, -3), jnp.where(turn == 0, 1 - core, core))
+        fold(6, (-3,), jnp.where(turn == 0, 1 - core, core))
 
         @pl.when(turn == 0)
         def _():
@@ -592,21 +622,31 @@
     share(0, half).wait_send()
     share(1, 1 - half).wait_send()
     for other_core in range(2):
-        direct_across(other_core).wait_send()
-
-        @pl.when(has_ahead)
-        def _():
-            direct_ahead(other_core).wait_send()
-            relay_across(other_core).wait_send()
-
-        @pl.when(has_behind)
-        def _():
-            direct_behind(other_core).wait_send()
-            relay_behind(other_core).wait_send()
-
-        @pl.when(has_ahead & has_behind)
-        def _():
-            relay_ahead(other_core).wait_send()
+        for local in range(blocks):
+            direct_across(other_core, local).wait_send()
+
+            @pl.when(has_ahead)
+            def _():
+                direct_ahead(other_core, local).wait_send()
+
+            @pl.when(has_behind)
+            def _():
+                direct_behind(other_core, local).wait_send()
+
+    @pl.when(has_ahead)
+    def _():
+        for index in range(slots):
+            relay_across(index).wait_send()
+
+    @pl.when(has_behind)
+    def _():
+        for index in range(reach):
+            relay_behind(index).wait_send()
+
+    @pl.when(has_ahead & has_behind)
+    def _():
+        for index in range(reach):
+            relay_ahead(index).wait_send()
 
     chip_stats.wait_send()
     pair_stats.wait_send()
@@ -646,7 +686,7 @@
             pltpu.SMEM(row_counts.shape, jnp.int32),
             pltpu.VMEM(embeddings.shape, wide),
             pltpu.VMEM((slots, rows, width), narrow),
-            pltpu.VMEM((7, 2, blocks, slice_rows, width), narrow),
+            pltpu.VMEM((7, slots, slice_rows, width), narrow),
             pltpu.VMEM((query_rows, 1), wide),
             pltpu.VMEM((query_rows, 1), wide),
             pltpu.VMEM((query_rows, width), wide),
@@ -659,7 +699,7 @@
             pltpu.VMEM((blocks, *stats), wide),
             pltpu.VMEM((blocks, *stats), wide),
             dma((4,)), dma((2,)), dma((2,)),
-            dma((3, 2)), dma((7, 2)), dma((3, 2)),
+            dma((3, 2, blocks)), dma((7, slots)), dma((3, slots)),
             dma((3,)), dma((3,)), dma((blocks + 1,)), dma((blocks + 1,)),
         ],
         compiler_params=pltpu.CompilerParams(
@@ -676,8 +716,11 @@
 def fits_kernel(block_shape):
     blocks, rows, width = block_shape
     covered = (SPAN + 2 * blocks - 2) // (2 * blocks) <= 3
+    far_enough = 3 * 2 * blocks >= SPAN
     whole_tiles = rows % 128 == 0 and width % 128 == 0
-    return lax.axis_size("pair") == 2 and lax.axis_size("own") % 4 == 0 and covered and whole_tiles
+    return lax.axis_size("pair") == 2 and lax.axis_size("own") % 4 == 0 and (
+        covered and far_enough and whole_tiles
+    )
 
 
 def device_part(embeddings, cluster_sizes, row_counts):

time: 35.1 us -> 34.7 us (0.989)
  the two profiles are of different devices: /device:TPU:10 before, /device:TPU:17 now
where the time goes in v3:
time: 34.7 us; the launch traced here: 34.6 us
  Pallas kernels  31.7 us (91%)
  local copies, waits for them, and re-layouts  2.24 us (6%)
  between operations  0.65 us (2%)
    pallas_call x1, Pallas kernels, kernel_body(): pl.pallas_call(functools.partial(kernel, groups, blocks, rows, slice_rows...  31.7 us
    unnamed x4, local copies, waits for them, and re-layouts  2.24 us

profile of v3, /device:TPU:17, one launch (start us, length us, event | category | flops | bytes accessed | tf_op | source)
XLA Modules:
  0.0 34.6 jit_solution(5022688700395038976)
XLA Ops:
  0.6 31.7 %shard_map.50 = (bf16[2,64,1024]{2,1,0:T(8,128)(2,1)}, f32[2,64]{1,0:T(2,128)}) custom-call(s32[8]{0:T(128)} %sizes_hbm.1, s32[32]{0:T(128)} %counts_hbm.1, f32[2,128,1024]{2,1,0:T(8,128)} %emb_hbm.1), custom_call_target="tpu_custom_call" | custom-call | flops 1879048192 | bytes 1048576 | tf_op jit(solution)/shard_map/pallas_call | solution.py:676
  32.3 0.0 copy-start
  32.3 1.7 %copy.7 = bf16[2,64,1024]{2,1,0:T(8,128)(2,1)} copy(bf16[2,64,1024]{2,1,0:T(8,128)(2,1)} %get-tuple-element.4) | data formatting | bytes 524288
  34.0 0.0 copy-done
  34.0 0.6 %copy.8 = f32[2,64]{1,0:T(2,128)} copy(f32[2,64]{1,0:T(2,128)S(1)} %copy-done) | data formatting | bytes 1024
Async XLA Ops:
  32.3 1.7 %copy-start = (f32[2,64]{1,0:T(2,128)S(1)}, f32[2,64]{1,0:T(2,128)}, u32[]{:S(2)}) copy-start(f32[2,64]{1,0:T(2,128)} %get-tuple-element.5) | copy-start | bytes 1540

commit v4 on v3

--- a/solution.py
+++ b/solution.py
@@ -469,6 +469,8 @@
 
     lax.fori_loop(0, 2, own_fold, 0)
 
+    early = slots // 2
+
     def pair_fold(turn, carry):
         @pl.when(turn == 0)
         def _():
@@ -476,7 +478,8 @@
             def _():
                 for index in range(slots):
                     arrived(2, (index + skip) % slots)
-                    relay_across(index).start()
+                    if index < early:
+                        relay_across(index).start()
 
             for index in range(reach):
                 arrived(1, lower(index))
@@ -486,6 +489,11 @@
                     relay_behind(index).start()
 
             arrived(1, lower(reach) % slots)
+
+        @pl.when((turn == 2) & has_ahead)
+        def _():
+            for index in range(early, slots):
+                relay_across(index).start()
 
         @pl.when((turn == 2) & has_behind)
         def _():

time: 34.7 us -> 34.7 us (level)
  no operation moved by 1% of the time
where the time goes in v4:
time: 34.7 us; the launch traced here: 34.6 us
  Pallas kernels  31.7 us (91%)
  local copies, waits for them, and re-layouts  2.24 us (6%)
  between operations  0.65 us (2%)
    pallas_call x1, Pallas kernels, kernel_body(): pl.pallas_call(functools.partial(kernel, groups, blocks, rows, slice_rows...  31.7 us
    unnamed x4, local copies, waits for them, and re-layouts  2.24 us

profile of v4, /device:TPU:17, one launch (start us, length us, event | category | flops | bytes accessed | tf_op | source)
XLA Modules:
  0.0 34.6 jit_solution(11290831175278248251)
XLA Ops:
  0.6 31.7 %shard_map.50 = (bf16[2,64,1024]{2,1,0:T(8,128)(2,1)}, f32[2,64]{1,0:T(2,128)}) custom-call(s32[8]{0:T(128)} %sizes_hbm.1, s32[32]{0:T(128)} %counts_hbm.1, f32[2,128,1024]{2,1,0:T(8,128)} %emb_hbm.1), custom_call_target="tpu_custom_call" | custom-call | flops 1879048192 | bytes 1048576 | tf_op jit(solution)/shard_map/pallas_call | solution.py:684
  32.3 0.0 copy-start
  32.4 1.7 %copy.7 = bf16[2,64,1024]{2,1,0:T(8,128)(2,1)} copy(bf16[2,64,1024]{2,1,0:T(8,128)(2,1)} %get-tuple-element.4) | data formatting | bytes 524288
  34.0 0.0 copy-done
  34.0 0.6 %copy.8 = f32[2,64]{1,0:T(2,128)} copy(f32[2,64]{1,0:T(2,128)S(1)} %copy-done) | data formatting | bytes 1024
Async XLA Ops:
  32.3 1.7 %copy-start = (f32[2,64]{1,0:T(2,128)S(1)}, f32[2,64]{1,0:T(2,128)}, u32[]{:S(2)}) copy-start(f32[2,64]{1,0:T(2,128)} %get-tuple-element.5) | copy-start | bytes 1540

commit v5 on v3

--- a/solution.py
+++ b/solution.py
@@ -459,6 +459,24 @@
                 weight, block_keys[:, columns], preferred_element_type=jnp.float32
             )
 
+    early = slots // 2
+
+    @pl.when(has_ahead)
+    def _():
+        for index in range(slots):
+            arrived(2, (index + skip) % slots)
+            if index < early:
+                relay_across(index).start()
+
+    for index in range(reach):
+        arrived(1, lower(index))
+
+        @pl.when(has_behind)
+        def _():
+            relay_behind(index).start()
+
+    arrived(1, lower(reach) % slots)
+
     share_in(0, half).wait_recv()
     keys[0] = queries[:, key_rows(core), :]
     share_in(1, 1 - half).wait_recv()
@@ -470,22 +488,10 @@
     lax.fori_loop(0, 2, own_fold, 0)
 
     def pair_fold(turn, carry):
-        @pl.when(turn == 0)
+        @pl.when((turn == 0) & has_ahead)
         def _():
-            @pl.when(has_ahead)
-            def _():
-                for index in range(slots):
-                    arrived(2, (index + skip) % slots)
-                    relay_across(index).start()
-
-            for index in range(reach):
-                arrived(1, lower(index))
-
-                @pl.when(has_behind)
-                def _():
-                    relay_behind(index).start()
-
-            arrived(1, lower(reach) % slots)
+            for index in range(early, slots):
+                relay_across(index).start()
 
         @pl.when((turn == 2) & has_behind)
         def _():

time: 34.7 us -> 34.7 us (level)
  no operation moved by 1% of the time
where the time goes in v5:
time: 34.7 us; the launch traced here: 34.6 us
  Pallas kernels  31.7 us (91%)
  local copies, waits for them, and re-layouts  2.24 us (6%)
  between operations  0.65 us (2%)
    pallas_call x1, Pallas kernels, kernel_body(): pl.pallas_call(functools.partial(kernel, groups, blocks, rows, slice_rows...  31.7 us
    unnamed x4, local copies, waits for them, and re-layouts  2.24 us

profile of v5, /device:TPU:17, one launch (start us, length us, event | category | flops | bytes accessed | tf_op | source)
XLA Modules:
  0.0 34.6 jit_solution(11742762719733019968)
XLA Ops:
  0.6 31.7 %shard_map.50 = (bf16[2,64,1024]{2,1,0:T(8,128)(2,1)}, f32[2,64]{1,0:T(2,128)}) custom-call(s32[8]{0:T(128)} %sizes_hbm.1, s32[32]{0:T(128)} %counts_hbm.1, f32[2,128,1024]{2,1,0:T(8,128)} %emb_hbm.1), custom_call_target="tpu_custom_call" | custom-call | flops 1879048192 | bytes 1048576 | tf_op jit(solution)/shard_map/pallas_call | solution.py:682
  32.3 0.0 copy-start
  32.3 1.7 %copy.7 = bf16[2,64,1024]{2,1,0:T(8,128)(2,1)} copy(bf16[2,64,1024]{2,1,0:T(8,128)(2,1)} %get-tuple-element.4) | data formatting | bytes 524288
  34.0 0.0 copy-done
  34.0 0.6 %copy.8 = f32[2,64]{1,0:T(2,128)} copy(f32[2,64]{1,0:T(2,128)S(1)} %copy-done) | data formatting | bytes 1024
Async XLA Ops:
  32.3 1.7 %copy-start = (f32[2,64]{1,0:T(2,128)S(1)}, f32[2,64]{1,0:T(2,128)}, u32[]{:S(2)}) copy-start(f32[2,64]{1,0:T(2,128)} %get-tuple-element.5) | copy-start | bytes 1540

commit v6 on v5

--- a/solution.py
+++ b/solution.py
@@ -459,14 +459,11 @@
                 weight, block_keys[:, columns], preferred_element_type=jnp.float32
             )
 
-    early = slots // 2
-
     @pl.when(has_ahead)
     def _():
         for index in range(slots):
             arrived(2, (index + skip) % slots)
-            if index < early:
-                relay_across(index).start()
+            relay_across(index).start()
 
     for index in range(reach):
         arrived(1, lower(index))
@@ -488,11 +485,6 @@
     lax.fori_loop(0, 2, own_fold, 0)
 
     def pair_fold(turn, carry):
-        @pl.when((turn == 0) & has_ahead)
-        def _():
-            for index in range(early, slots):
-                relay_across(index).start()
-
         @pl.when((turn == 2) & has_behind)
         def _():
             for index in range(reach):

time: 34.7 us -> 34.7 us (level)
  no operation moved by 1% of the time
where the time goes in v6:
time: 34.7 us; the launch traced here: 34.6 us
  Pallas kernels  31.7 us (91%)
  local copies, waits for them, and re-layouts  2.24 us (6%)
  between operations  0.65 us (2%)
    pallas_call x1, Pallas kernels, kernel_body(): pl.pallas_call(functools.partial(kernel, groups, blocks, rows, slice_rows...  31.7 us
    unnamed x4, local copies, waits for them, and re-layouts  2.24 us

profile of v6, /device:TPU:17, one launch (start us, length us, event | category | flops | bytes accessed | tf_op | source)
XLA Modules:
  0.0 34.6 jit_solution(456794894381220055)
XLA Ops:
  0.6 31.7 %shard_map.50 = (bf16[2,64,1024]{2,1,0:T(8,128)(2,1)}, f32[2,64]{1,0:T(2,128)}) custom-call(s32[8]{0:T(128)} %sizes_hbm.1, s32[32]{0:T(128)} %counts_hbm.1, f32[2,128,1024]{2,1,0:T(8,128)} %emb_hbm.1), custom_call_target="tpu_custom_call" | custom-call | flops 1879048192 | bytes 1048576 | tf_op jit(solution)/shard_map/pallas_call | solution.py:674
  32.3 0.0 copy-start
  32.3 1.7 %copy.7 = bf16[2,64,1024]{2,1,0:T(8,128)(2,1)} copy(bf16[2,64,1024]{2,1,0:T(8,128)(2,1)} %get-tuple-element.4) | data formatting | bytes 524288
  34.0 0.0 copy-done
  34.0 0.6 %copy.8 = f32[2,64]{1,0:T(2,128)} copy(f32[2,64]{1,0:T(2,128)S(1)} %copy-done) | data formatting | bytes 1024
Async XLA Ops:
  32.3 1.7 %copy-start = (f32[2,64]{1,0:T(2,128)S(1)}, f32[2,64]{1,0:T(2,128)}, u32[]{:S(2)}) copy-start(f32[2,64]{1,0:T(2,128)} %get-tuple-element.5) | copy-start | bytes 1540
